TPU v7x, 256 devices: a whole 4x4x8 slice. The times are simulated.
256 devices in a mesh: grp: 8 (over y, core), sp: 32 (over z, x).
Axes of the slice: x: 4, y: 4, z: 8, core: 2. Of those that a mesh axis runs over, the one named last changes fastest.
Arguments:
- query: bfloat16 [32768, 4096], P(('grp', 'sp')), parts along dimension 0, may hold values from -24 to 24
- keys: bfloat16 [32768, 512], P(('grp', 'sp')), parts along dimension 0, may hold values from -4 to 4
- values: bfloat16 [32768, 512], P(('grp', 'sp')), parts along dimension 0, may hold values from -6 to 6
- out_grad: bfloat16 [32768, 4096], P(('grp', 'sp')), parts along dimension 0, may hold values from -6 to 6
- documents: int32 [32768], P(('grp', 'sp')), parts along dimension 0, may hold values from 0 to 7, never falling along the last dimension, each value on 1 to 2048 neighbouring positions
Outputs:
- attn_out: bfloat16 [32768, 4096], P(('grp', 'sp')), parts along dimension 0
- query_grad: bfloat16 [32768, 4096], P(('grp', 'sp')), parts along dimension 0
- key_grad: bfloat16 [32768, 512], P(('grp', 'sp')), parts along dimension 0
- value_grad: bfloat16 [32768, 512], P(('grp', 'sp')), parts along dimension 0
There are 8 independent parts, one for each index of `grp`. A program takes and returns all parts, laid end to end along the dimension named above; each array names one. Nothing has to cross between parts.
Inputs may be any that keep to these rules, and one draw needn't show every extreme that they name: `documents`: document ids never fall along the window; each document holds 1 to 2048 tokens and one holds exactly 2048.
All inputs are finite; a program needn't handle non-finite values.
Results may differ from a plain program's by a relative error of at most 0.019.
Values may be sent and summed in bfloat16 or wider, within the bound.
A program may use at most 128 MiB of HBM per device.

v0:
```python
import math

import jax
import jax.numpy as jnp
from jax import lax
from jax.experimental import pallas as pl
from jax.experimental.pallas import tpu as pltpu
from jax.sharding import PartitionSpec as P

HD = 128
TOK = 128
NX = 4
NZ = 8
GROUP = 8
ROWS = NX * TOK
HALF = ROWS // 2
FAR = 4
WIDE = GROUP * HD
UNROLL = 4
PAD = 16
BIG = float(2**20)
LOW = -1e30
SCALE = 1.0 / math.sqrt(HD)
LOG2E = math.log2(math.e)
MESH = pl.DeviceIdType.MESH
F32, BF16 = jnp.float32, jnp.bfloat16

I_Q0, I_Q1, I_G0, I_G1, I_O0, I_O1 = range(6)
I_DQ = 6
QUARTERS = 4
I_K, I_V, I_DOC, I_DK, I_DV = range(10, 15)
ITEMS = 15


def dot_nn(a, b):
    return lax.dot_general(a, b, (((1,), (0,)), ((), ())), preferred_element_type=F32)


def kernel(
    q_hbm, k_hbm, v_hbm, g_hbm, doc_in, o_out, dq_out, dk_out, dv_out,
    kbuf, vbuf, dbuf, dstage, kext, qext, kt, vt, qbuf, gbuf, qt, gt, pbuf,
    mrow, mblk, delta, linv, ot, dqt, dkacc, dvacc, obuf, dqbuf, rbuf, sbuf, fbuf,
    xs, xr, zs, zr, rs, rr,
):
    me = lax.axis_index("sp")
    z = me // NX
    x = me % NX
    up = ((z + 1) % NZ) * NX + x
    down = ((z + NZ - 1) % NZ) * NX + x

    def peer(d):
        return (x + d) % NX

    def xid(d):
        return z * NX + peer(d)

    def cols(i, width):
        return pl.ds(pl.multiple_of(i * width, HD), width)

    def head(h):
        return pl.ds(pl.multiple_of(h * HD, HD), HD)

    def xrefs(item, to, at):
        if not isinstance(item, int) or item < I_K:
            size = WIDE // 2 if isinstance(item, int) and item < I_DQ else WIDE // QUARTERS
            part = pl.multiple_of((item - I_DQ) * size, HD) if size != WIDE // 2 else (item % 2) * size

            def outer(ref, i):
                return ref.at[:, pl.ds(pl.multiple_of(i * WIDE + part, HD), size)]

            def inner(ref, i):
                return ref.at[i, :, pl.ds(part, size)]

            if size != WIDE // 2:
                return inner(dqbuf, to), outer(dq_out, at)
            if item in (I_Q0, I_Q1):
                return outer(q_hbm, to), inner(qbuf, at)
            if item in (I_G0, I_G1):
                return outer(g_hbm, to), inner(gbuf, at)
            return inner(obuf, to), outer(o_out, at)
        if item == I_K:
            return k_hbm.at[:, cols(to, HD)], kbuf.at[0, at]
        if item == I_V:
            return v_hbm.at[:, cols(to, HD)], vbuf.at[0, at]
        if item == I_DOC:
            return dstage, dbuf.at[0, at]
        if item == I_DK:
            return fbuf.at[0, to], dk_out.at[:, cols(at, HD)]
        return fbuf.at[1, to], dv_out.at[:, cols(at, HD)]

    def remote(src, dst, send, recv, other):
        return pltpu.make_async_remote_copy(
            src_ref=src, dst_ref=dst, send_sem=send, recv_sem=recv, device_id={"sp": other}, device_id_type=MESH
        )

    def xcopy(item, d, sending=True):
        src, dst = xrefs(item, peer(d), x if sending else peer(NX - d))
        return remote(src, dst, xs.at[item, d], xr.at[item, d], xid(d))

    def xlocal(item):
        src, dst = xrefs(item, x, x)
        return pltpu.make_async_copy(src, dst, xr.at[item, 0])

    def xsend(item):
        for d in (1, 3, 2):
            xcopy(item, d).start()

    def xrecv(item):
        xlocal(item).wait()
        for d in (1, 3, 2):
            xcopy(item, d, sending=False).wait_recv()

    def xsent(item):
        for d in (1, 3, 2):
            xcopy(item, d).wait_send()

    def zcopy(far, item):
        buf = (kbuf, vbuf, dbuf)[item]
        return pltpu.make_async_remote_copy(
            src_ref=buf.at[far], dst_ref=buf.at[far + 1], send_sem=zs.at[far, item], recv_sem=zr.at[far, item],
            device_id={"sp": up}, device_id_type=MESH,
        )

    def rcopy(far, half):
        return pltpu.make_async_remote_copy(
            src_ref=sbuf.at[far - 1, half], dst_ref=rbuf.at[far - 1, half],
            send_sem=rs.at[far - 1, half], recv_sem=rr.at[far - 1, half],
            device_id={"sp": down}, device_id_type=MESH,
        )

    dstage[...] = jnp.broadcast_to(doc_in[...], (8, TOK))
    for item in (I_K, I_V, I_DOC, I_Q0, I_Q1, I_G0, I_G1):
        xlocal(item).start()

    barrier = pltpu.get_barrier_semaphore()
    for other in (xid(1), xid(2), xid(3), up, down):
        pl.semaphore_signal(barrier, inc=1, device_id={"sp": other}, device_id_type=MESH)
    pl.semaphore_wait(barrier, 5)

    for item in (I_K, I_V, I_DOC):
        xsend(item)

    mrow[...] = jnp.full(mrow.shape, LOW, F32)
    for far in range(FAR + 1):
        vt[far, HD:, :] = jnp.ones((PAD, ROWS), BF16)

    def zero_head(h, _):
        ot[h] = jnp.zeros((HD + PAD, ROWS), F32)
        dqt[h] = jnp.zeros((HD, ROWS), F32)
        return 0

    lax.fori_loop(0, GROUP, zero_head, 0)

    def prepare(far):
        line = lax.broadcasted_iota(jnp.int32, (TOK, TOK), 0)
        for b in range(NX):
            bias = jnp.where((line == dbuf[far, b][0:1, :]) | (line >= 8), 0.0, -BIG).astype(F32)
            kext[far, b * TOK:(b + 1) * TOK, :] = bias.T.astype(BF16)
            kt[far, :, b * TOK:(b + 1) * TOK] = kbuf[far, b].T
            vt[far, :HD, b * TOK:(b + 1) * TOK] = vbuf[far, b].T

    def rows_in(buf, h, first, count):
        return buf[first // TOK:(first + count) // TOK, :, head(h)].reshape(count, HD)

    def turn(src, dst, h0, count):
        def step(i, _):
            for h in (h0 + 2 * i, h0 + 2 * i + 1):
                for b in range(NX):
                    dst[h, :, b * TOK:(b + 1) * TOK] = src[b, :, head(h)].T
            return 0
        lax.fori_loop(0, count // 2, step, 0)

    def over_heads(body, h0, count, together):
        def step(i, _):
            body([h0 + i * together + u for u in range(together)])
            return 0
        if count == together:
            step(0, 0)
        else:
            lax.fori_loop(0, count // together, step, 0)

    def forward(far, key0, count, first, rows, h0, heads_in, causal=False):
        span, some = slice(first, first + rows), slice(key0, key0 + count)

        def body(heads):
            keys = jnp.concatenate(
                [kbuf[far, key0 // TOK:(key0 + count) // TOK].reshape(count, HD), kext[far, some, :]], axis=1
            )
            ext = qext[:, span]
            values_t = vt[far, :, some]
            old = [(mrow[h, :, span], ot[h, :, span]) for h in heads]
            scores = [dot_nn(keys, jnp.concatenate([qt[h, :, span], ext], axis=0)) for h in heads]
            if causal:
                key_at = lax.broadcasted_iota(jnp.int32, (count, rows), 0) + key0
                row_at = lax.broadcasted_iota(jnp.int32, (count, rows), 1) + first
                scores = [jnp.where(key_at <= row_at, s, LOW) for s in scores]
            new = []
            for s, (m_old, o_old) in zip(scores, old):
                m_new = jnp.maximum(m_old, jnp.max(s, axis=0, keepdims=True))
                pb = jnp.exp2((s - m_new) * (SCALE * LOG2E)).astype(BF16)
                alpha = jnp.exp2((m_old - m_new) * (SCALE * LOG2E))
                new.append((m_new, o_old * alpha + dot_nn(values_t, pb), pb))
            for h, (m_new, o_new, pb) in zip(heads, new):
                mrow[h, :, span] = m_new
                for half in range(key0 // HALF, (key0 + count) // HALF):
                    mblk[far, half, h, :, span] = m_new
                ot[h, :, span] = o_new
                pbuf[far, h, some, span] = pb

        over_heads(body, h0, heads_in, UNROLL)

    def gradients(tiles, heads):
        loaded = []
        for far, half, first, rows, slot in tiles:
            span = slice(first, first + rows)
            some = pl.ds(half * HALF if isinstance(half, int) else pl.multiple_of(half * HALF, HALF), HALF)
            loaded.append((
                vbuf[far, pl.ds(2 * half, 2)].reshape(HALF, HD),
                kt[far, :, some],
                [(jnp.exp2((mblk[far, half, h, :, span] - mrow[h, :, span]) * (SCALE * LOG2E)) * linv[h, :, span]
                  ).astype(BF16) for h in heads],
                [pbuf[far, h, some, span] for h in heads],
                dvacc[slot], dkacc[slot],
            ))
        grads = [rows_in(gbuf, h, 0, ROWS) for h in heads]
        queries = [rows_in(qbuf, h, 0, ROWS) for h in heads]
        grads_t = [gt[h] for h in heads]
        deltas = [delta[h] for h in heads]
        dq = [dqt[h] for h in heads]
        pushed = [
            [dot_nn(t[0], g[:, first:first + rows]) for g in grads_t]
            for t, (_, _, first, rows, _) in zip(loaded, tiles)
        ]
        sums = []
        for t, pushes, (_, _, first, rows, _) in zip(loaded, pushed, tiles):
            _, keys_t, factor, shares, dv_old, dk_old = t
            span = slice(first, first + rows)
            weights, slopes = [], []
            for i in range(len(heads)):
                weights.append(shares[i] * factor[i])
                slopes.append(weights[i] * (pushes[i] - deltas[i][:, span]).astype(BF16))
                term = dot_nn(keys_t, slopes[i])
                parts = [dq[i][:, :first]] if first else []
                parts.append(dq[i][:, span] + term)
                if first + rows < ROWS:
                    parts.append(dq[i][:, first + rows:])
                dq[i] = parts[0] if len(parts) == 1 else jnp.concatenate(parts, axis=1)
            sums.append((
                dv_old + dot_nn(jnp.concatenate(weights, axis=1), jnp.concatenate([g[span] for g in grads], axis=0)),
                dk_old + dot_nn(jnp.concatenate(slopes, axis=1), jnp.concatenate([q[span] for q in queries], axis=0)),
            ))
        for (_, _, _, _, slot), (dv, dk) in zip(tiles, sums):
            dvacc[slot] = dv
            dkacc[slot] = dk
        return dq

    def backward(far, half, first, rows, heads):
        for h, dq in zip(heads, gradients([(far, half, first, rows, half)], heads)):
            dqt[h] = dq

    def arrive(far, items):
        @pl.when(z >= far)
        def _():
            for item in items:
                zcopy(far - 1, item).wait_recv()

                if not (isinstance(far, int) and far == FAR):
                    @pl.when(z < NZ - 1)
                    def _():
                        zcopy(far, item).start()

    for item, own in enumerate((I_K, I_V, I_DOC)):
        xrecv(own)

        @pl.when(z < NZ - 1)
        def _():
            zcopy(0, item).start()

    xsend(I_Q0)
    prepare(0)
    line = lax.broadcasted_iota(jnp.int32, (HD, TOK), 0)
    for b in range(NX):
        qext[:, b * TOK:(b + 1) * TOK] = jnp.where(line == dbuf[0, b][0:1, :], 1.0, 0.0).astype(BF16)
    arrive(1, (0, 1, 2))

    def own_row(part):
        h0 = part * (GROUP // 2)
        xrecv(I_Q0 + part)
        if part == 0:
            xsend(I_Q1)
        else:
            xsend(I_G0)
            xsend(I_G1)
        turn(qbuf, qt, h0, GROUP // 2)
        forward(0, 0, HALF, 0, ROWS, h0, GROUP // 2, causal=True)
        forward(0, HALF, HALF, HALF, HALF, h0, GROUP // 2, causal=True)

    own_row(0)

    def forward_step(i, _):
        late = i // 4
        far = (1 - late) * (1 + i % 2) + late * 3
        part = (1 - late) * (i // 2) + late * (i - 4)

        @pl.when(i == 0)
        def _():
            arrive(2, (0,))

        @pl.when(i == 1)
        def _():
            arrive(2, (1, 2))

        @pl.when(i == 2)
        def _():
            arrive(3, (0,))
            own_row(1)
            arrive(3, (1, 2))

        @pl.when(((i < 2) | (i == 4)) & (z >= far))
        def _():
            prepare(far)

        @pl.when(z >= far)
        def _():
            forward(far, 0, ROWS, 0, ROWS, part * (GROUP // 2), GROUP // 2)
        return 0

    lax.fori_loop(0, 2 * (FAR - 1), forward_step, 0)
    xrecv(I_G0)
    turn(gbuf, gt, 0, GROUP // 2)
    arrive(FAR, (0, 1, 2))

    @pl.when(z >= FAR)
    def _():
        prepare(FAR)
        forward(FAR, 0, HALF, 0, HALF, 0, GROUP)
        forward(FAR, HALF, HALF, 0, ROWS, 0, GROUP)

    xrecv(I_G1)
    turn(gbuf, gt, GROUP // 2, GROUP // 2)

    def finish(i, _):
        for h in [4 * i + u for u in range(4)]:
            inverse = 1.0 / ot[h, HD:HD + 1, :]
            linv[h] = inverse
            out = (ot[h, :HD, :] * inverse).astype(BF16)
            delta[h] = jnp.sum(out.astype(F32) * gt[h].astype(F32), axis=0, keepdims=True)
            for b in range(NX):
                obuf[b, :, head(h)] = out[:, b * TOK:(b + 1) * TOK].T
        return 0

    lax.fori_loop(0, GROUP // 4, finish, 0)
    for item in (I_O0, I_O1):
        xlocal(item).start()
        xsend(item)

    everyone = list(range(GROUP))

    def clear(slot):
        dkacc[slot] = jnp.zeros((HALF, HD), F32)
        dvacc[slot] = jnp.zeros((HALF, HD), F32)

    def add_above(far, half, slot):
        @pl.when(z < NZ - 1)
        def _():
            rcopy(far + 1, half).wait_recv()
            dkacc[slot] = dkacc[slot] + rbuf[far, half, 0].astype(F32)
            dvacc[slot] = dvacc[slot] + rbuf[far, half, 1].astype(F32)

    def send_down(far, half):
        sbuf[far - 1, half, 0] = dkacc[half].astype(BF16)
        sbuf[far - 1, half, 1] = dvacc[half].astype(BF16)
        rcopy(far, half).start()

    @pl.when(z >= FAR)
    def _():
        clear(0)
        backward(FAR, 0, 0, HALF, everyone)
        send_down(FAR, 0)

    def backward_step(i, _):
        far, half = (2 * FAR - i) // 2, (i + 1) % 2

        @pl.when(z >= far)
        def _():
            clear(half)
            backward(far, half, 0, ROWS, everyone)

            @pl.when(far < FAR)
            def _():
                add_above(far, half, half)

            send_down(far, half)
        return 0

    lax.fori_loop(0, 2 * FAR - 2, backward_step, 0)

    for slot in (1, 2, 3):
        clear(slot)
    last = (1, 1, 0, ROWS, 1)
    own = [(0, 0, 0, ROWS, 2), (0, 1, HALF, HALF, 3)]
    pair = GROUP // QUARTERS

    def finish_dq(g, tiles):
        heads = [g * pair + u for u in range(pair)]
        for h, dq in zip(heads, gradients(tiles, heads)):
            dq = (dq * SCALE).astype(BF16)
            for b in range(NX):
                dqbuf[b, :, head(h)] = dq[:, b * TOK:(b + 1) * TOK].T
        xlocal(I_DQ + g).start()
        xsend(I_DQ + g)

    @pl.when(z >= 1)
    def _():
        def step(g, _):
            finish_dq(g, [last] + own)
            return 0
        lax.fori_loop(0, QUARTERS - 1, step, 0)
        backward(1, 1, 0, ROWS, everyone[-pair:])
        add_above(1, 1, 1)
        send_down(1, 1)

    @pl.when(z == 0)
    def _():
        def step(g, _):
            finish_dq(g, own)
            return 0
        lax.fori_loop(0, QUARTERS - 1, step, 0)

    finish_dq(QUARTERS - 1, own)
    for half in range(2):
        add_above(0, half, 2 + half)
        fbuf[0, 2 * half:2 * half + 2] = (dkacc[2 + half] * SCALE).astype(BF16).reshape(2, TOK, HD)
        fbuf[1, 2 * half:2 * half + 2] = dvacc[2 + half].astype(BF16).reshape(2, TOK, HD)
        for item in (I_DK, I_DV):
            @pl.when(x // 2 == half)
            def _():
                xlocal(item).start()
            for d in (1, 3, 2):
                @pl.when(peer(d) // 2 == half)
                def _():
                    xcopy(item, d).start()

    for item in [I_O0, I_O1, I_DK, I_DV] + [I_DQ + g for g in range(QUARTERS)]:
        xrecv(item)
    for item in range(ITEMS):
        xsent(item)
    for far in range(FAR):
        @pl.when((z >= far) & (z < NZ - 1))
        def _():
            for item in range(3):
                zcopy(far, item).wait_send()
    for far in range(1, FAR + 1):
        @pl.when(z >= far)
        def _():
            for half in range(2):
                rcopy(far, half).wait_send()


def hand_over(*refs):
    sources, targets, held, sems = refs[:4], refs[4:8], refs[8:12], refs[12]
    loads = [pltpu.make_async_copy(a, b, sems.at[0, i]) for i, (a, b) in enumerate(zip(sources, held))]
    stores = [pltpu.make_async_copy(a, b, sems.at[1, i]) for i, (a, b) in enumerate(zip(held, targets))]
    for load in loads:
        load.start()
    for load, store in zip(loads, stores):
        load.wait()
        store.start()
    for store in stores:
        store.wait()


def per_device(query, keys, values, out_grad, documents):
    wide, narrow = query.shape, keys.shape
    hbm = pl.BlockSpec(memory_space=pl.ANY)
    vmem = pltpu.VMEM
    dma = pltpu.SemaphoreType.DMA
    results = pl.pallas_call(
        kernel,
        out_shape=(
            jax.ShapeDtypeStruct(wide, BF16),
            jax.ShapeDtypeStruct(wide, BF16),
            jax.ShapeDtypeStruct(narrow, BF16),
            jax.ShapeDtypeStruct(narrow, BF16),
        ),
        in_specs=[hbm, hbm, hbm, hbm, pl.BlockSpec(memory_space=pltpu.VMEM)],
        out_specs=(hbm, hbm, hbm, hbm),
        scratch_shapes=[
            vmem((FAR + 1, NX, TOK, HD), BF16),
            vmem((FAR + 1, NX, TOK, HD), BF16),
            vmem((FAR + 1, NX, 8, TOK), jnp.int32),
            vmem((8, TOK), jnp.int32),
            vmem((FAR + 1, ROWS, HD), BF16),
            vmem((HD, ROWS), BF16),
            vmem((FAR + 1, HD, ROWS), BF16),
            vmem((FAR + 1, HD + PAD, ROWS), BF16),
            vmem((NX, TOK, WIDE), BF16),
            vmem((NX, TOK, WIDE), BF16),
            vmem((GROUP, HD, ROWS), BF16),
            vmem((GROUP, HD, ROWS), BF16),
            vmem((FAR + 1, GROUP, ROWS, ROWS), BF16),
            vmem((GROUP, 1, ROWS), F32),
            vmem((FAR + 1, 2, GROUP, 1, ROWS), F32),
            vmem((GROUP, 1, ROWS), F32),
            vmem((GROUP, 1, ROWS), F32),
            vmem((GROUP, HD + PAD, ROWS), F32),
            vmem((GROUP, HD, ROWS), F32),
            vmem((4, HALF, HD), F32),
            vmem((4, HALF, HD), F32),
            vmem((NX, TOK, WIDE), BF16),
            vmem((NX, TOK, WIDE), BF16),
            vmem((FAR, 2, 2, HALF, HD), BF16),
            vmem((FAR, 2, 2, HALF, HD), BF16),
            vmem((2, NX, TOK, HD), BF16),
            dma((ITEMS, NX)), dma((ITEMS, NX)),
            dma((FAR, 3)), dma((FAR, 3)),
            dma((FAR, 2)), dma((FAR, 2)),
        ],
        compiler_params=pltpu.CompilerParams(
            collective_id=0, has_side_effects=True, vmem_limit_bytes=56 * 2**20
        ),
        cost_estimate=pl.CostEstimate(flops=13 * 10**9, bytes_accessed=9 * 2**20, transcendentals=9 * 10**6),
        name="attention_both_ways",
    )(query, keys, values, out_grad, documents.reshape(1, TOK))
    return pl.pallas_call(
        hand_over,
        out_shape=tuple(jax.ShapeDtypeStruct(r.shape, r.dtype) for r in results),
        in_specs=[hbm] * 4,
        out_specs=(hbm,) * 4,
        scratch_shapes=[vmem(r.shape, r.dtype) for r in results] + [dma((2, 4))],
        compiler_params=pltpu.CompilerParams(vmem_limit_bytes=56 * 2**20),
        cost_estimate=pl.CostEstimate(flops=0, bytes_accessed=5 * 2**20, transcendentals=0),
        name="hand_over",
    )(*results)


def solution(mesh):
    spec = P(("grp", "sp"), None)
    return jax.shard_map(
        per_device,
        mesh=mesh,
        in_specs=(spec, spec, spec, spec, P(("grp", "sp"))),
        out_specs=(spec, spec, spec, spec),
        check_vma=False,
    )
```

profile of v0, /device:TPU:86, one launch (start us, length us, event | category | flops | bytes accessed | tf_op | source)
XLA Modules:
  0.0 79.5 jit_solution(8933492178444120075)
XLA Ops:
  0.6 76.0 %attention_both_ways.1 = (bf16[128,4096]{1,0:T(8,128)(2,1)}, bf16[128,4096]{1,0:T(8,128)(2,1)}, bf16[128,512]{1,0:T(8,128)(2,1)}, bf16[128,512]{1,0:T(8,128)(2,1)}) custom-call(bf16[128,4096]{1,0:T(8,128)(2,1)} %q_hbm.1, bf16[128,512]{1,0:T(8,128)(2,1)} %k_hbm.1, bf16[128,512]{1,0:T(8,128)(2,1)} %v_hbm.1, bf16[128,4096]{1,0:T(8,128)(2,1)} %g_hbm.1, ...), custom_call_target="tpu_custom_call" | custom-call | flops 12999999488 | bytes 9437184 | tf_op jit(solution)/shard_map/attention_both_ways/pallas_call | solution.py:478
  76.7 2.7 %hand_over.1 = (bf16[128,4096]{1,0:T(8,128)(2,1)}, bf16[128,4096]{1,0:T(8,128)(2,1)}, bf16[128,512]{1,0:T(8,128)(2,1)}, bf16[128,512]{1,0:T(8,128)(2,1)}) custom-call(bf16[128,4096]{1,0:T(8,128)(2,1)} %get-tuple-element.8.refs_0_, bf16[128,4096]{1,0:T(8,128)(2,1)} %get-tuple-element.9.refs_1_, bf16[128,512]{1,0:T(8,128)(2,1)} %get-tuple-element.10.refs_2_, ...), custom_call_target="tpu_custom_call" | custom-call | bytes 5242880 | tf_op jit(solution)/shard_map/hand_over/pallas_call | solution.py:525
where the time goes:
time: 79.6 us; the launch traced here: 79.5 us
  Pallas kernels  78.7 us (99%)
  between operations  0.8 us (1%)
    pallas_call x1, Pallas kernels, per_device(): pl.pallas_call(kernel, out_shape=(jax.ShapeDtypeStruct(wide, BF16), jax.S...  76 us
    pallas_call x1, Pallas kernels, per_device(): pl.pallas_call(hand_over, out_shape=tuple((jax.ShapeDtypeStruct(r.shape,...  2.68 us

commit v1 on v0

--- a/solution.py
+++ b/solution.py
@@ -227,28 +227,37 @@
         grads_t = [gt[h] for h in heads]
         deltas = [delta[h] for h in heads]
         dq = [dqt[h] for h in heads]
-        pushed = [
-            [dot_nn(t[0], g[:, first:first + rows]) for g in grads_t]
-            for t, (_, _, first, rows, _) in zip(loaded, tiles)
-        ]
-        sums = []
-        for t, pushes, (_, _, first, rows, _) in zip(loaded, pushed, tiles):
-            _, keys_t, factor, shares, dv_old, dk_old = t
+        units = [(t, pair) for t in range(len(tiles)) for pair in zip(range(0, len(heads), 2), range(1, len(heads), 2))]
+
+        def push(unit):
+            t, pair = unit
+            _, _, first, rows, _ = tiles[t]
+            return [dot_nn(loaded[t][0], grads_t[i][:, first:first + rows]) for i in pair]
+
+        sums = [(t[4], t[5]) for t in loaded]
+        pushed = [push(unit) for unit in units[:2]]
+        for n, (t, pair) in enumerate(units):
+            _, keys_t, factor, shares, _, _ = loaded[t]
+            _, _, first, rows, _ = tiles[t]
             span = slice(first, first + rows)
             weights, slopes = [], []
-            for i in range(len(heads)):
-                weights.append(shares[i] * factor[i])
-                slopes.append(weights[i] * (pushes[i] - deltas[i][:, span]).astype(BF16))
-                term = dot_nn(keys_t, slopes[i])
+            for i, pushes in zip(pair, pushed[n]):
+                w = shares[i] * factor[i]
+                weights.append(w)
+                slopes.append(w * (pushes - deltas[i][:, span]).astype(BF16))
+            if n + 2 < len(units):
+                pushed.append(push(units[n + 2]))
+            for i, slope in zip(pair, slopes):
                 parts = [dq[i][:, :first]] if first else []
-                parts.append(dq[i][:, span] + term)
+                parts.append(dq[i][:, span] + dot_nn(keys_t, slope))
                 if first + rows < ROWS:
                     parts.append(dq[i][:, first + rows:])
                 dq[i] = parts[0] if len(parts) == 1 else jnp.concatenate(parts, axis=1)
-            sums.append((
-                dv_old + dot_nn(jnp.concatenate(weights, axis=1), jnp.concatenate([g[span] for g in grads], axis=0)),
-                dk_old + dot_nn(jnp.concatenate(slopes, axis=1), jnp.concatenate([q[span] for q in queries], axis=0)),
-            ))
+            dv, dk = sums[t]
+            sums[t] = (
+                dv + dot_nn(jnp.concatenate(weights, axis=1), jnp.concatenate([grads[i][span] for i in pair], axis=0)),
+                dk + dot_nn(jnp.concatenate(slopes, axis=1), jnp.concatenate([queries[i][span] for i in pair], axis=0)),
+            )
         for (_, _, _, _, slot), (dv, dk) in zip(tiles, sums):
             dvacc[slot] = dv
             dkacc[slot] = dk
@@ -393,9 +402,9 @@
             send_down(far, half)
         return 0
 
-    lax.fori_loop(0, 2 * FAR - 2, backward_step, 0)
-
-    for slot in (1, 2, 3):
+    lax.fori_loop(0, 2 * FAR - 3, backward_step, 0)
+
+    for slot in range(4):
         clear(slot)
     last = (1, 1, 0, ROWS, 1)
     own = [(0, 0, 0, ROWS, 2), (0, 1, HALF, HALF, 3)]
@@ -412,10 +421,15 @@
 
     @pl.when(z >= 1)
     def _():
+        finish_dq(0, [(1, 0, 0, ROWS, 0), last] + own)
+        backward(1, 0, 0, ROWS, everyone[pair:])
+        add_above(1, 0, 0)
+        send_down(1, 0)
+
         def step(g, _):
             finish_dq(g, [last] + own)
             return 0
-        lax.fori_loop(0, QUARTERS - 1, step, 0)
+        lax.fori_loop(1, QUARTERS - 1, step, 0)
         backward(1, 1, 0, ROWS, everyone[-pair:])
         add_above(1, 1, 1)
         send_down(1, 1)

time: 79.6 us -> 79.5 us (level)
  no operation moved by 1% of the time
where the time goes in v1:
time: 79.5 us; the launch traced here: 79.4 us
  Pallas kernels  78.6 us (99%)
  between operations  0.82 us (1%)
    pallas_call x1, Pallas kernels, per_device(): pl.pallas_call(kernel, out_shape=(jax.ShapeDtypeStruct(wide, BF16), jax.S...  75.9 us
    pallas_call x1, Pallas kernels, per_device(): pl.pallas_call(hand_over, out_shape=tuple((jax.ShapeDtypeStruct(r.shape,...  2.68 us

profile of v1, /device:TPU:86, one launch (start us, length us, event | category | flops | bytes accessed | tf_op | source)
XLA Modules:
  0.0 79.4 jit_solution(264525506979893534)
XLA Ops:
  0.6 75.9 %attention_both_ways.1 = (bf16[128,4096]{1,0:T(8,128)(2,1)}, bf16[128,4096]{1,0:T(8,128)(2,1)}, bf16[128,512]{1,0:T(8,128)(2,1)}, bf16[128,512]{1,0:T(8,128)(2,1)}) custom-call(bf16[128,4096]{1,0:T(8,128)(2,1)} %q_hbm.1, bf16[128,512]{1,0:T(8,128)(2,1)} %k_hbm.1, bf16[128,512]{1,0:T(8,128)(2,1)} %v_hbm.1, bf16[128,4096]{1,0:T(8,128)(2,1)} %g_hbm.1, ...), custom_call_target="tpu_custom_call" | custom-call | flops 12999999488 | bytes 9437184 | tf_op jit(solution)/shard_map/attention_both_ways/pallas_call | solution.py:492
  76.5 2.7 %hand_over.1 = (bf16[128,4096]{1,0:T(8,128)(2,1)}, bf16[128,4096]{1,0:T(8,128)(2,1)}, bf16[128,512]{1,0:T(8,128)(2,1)}, bf16[128,512]{1,0:T(8,128)(2,1)}) custom-call(bf16[128,4096]{1,0:T(8,128)(2,1)} %get-tuple-element.8.refs_0_, bf16[128,4096]{1,0:T(8,128)(2,1)} %get-tuple-element.9.refs_1_, bf16[128,512]{1,0:T(8,128)(2,1)} %get-tuple-element.10.refs_2_, ...), custom_call_target="tpu_custom_call" | custom-call | bytes 5242880 | tf_op jit(solution)/shard_map/hand_over/pallas_call | solution.py:539
